TPU v7x, 32 devices: a whole 2x2x4 slice. The times are simulated.
32 devices in a mesh: dp: 4 (over z), row: 2 (over core), col: 4 (over y, x).
Axes of the slice: x: 2, y: 2, z: 4, core: 2. Of those that a mesh axis runs over, the one named last changes fastest.
Arguments:
- features: bfloat16 [2048, 4096], P(('dp', 'row')), may hold values from -6 to 6
- w_in: bfloat16 [4096, 4096], P('row', 'col'), may hold values from -0.09375 to 0.09375
- w_out: bfloat16 [4096, 1024], P('col'), may hold values from -0.09375 to 0.09375
- captions: bfloat16 [2048, 1024], P(('dp', 'row', 'col')), may hold values from -6 to 6
- positive: int32 [2048], P(('dp', 'row')), may hold values from 0 to 2047, each once
Outputs:
- fig_terms: float32 [2048], P(('dp', 'row'))
- cap_terms: float32 [2048], P(('dp', 'row', 'col'))
- grad_w_in: float32 [4096, 4096], P(('dp', 'row'), 'col')
- grad_w_out: float32 [4096, 1024], P('col', ('dp', 'row'))
Inputs may be any that keep to these rules, and one draw needn't show every extreme that they name: positive is a permutation: every caption is the match of exactly one figure.
All inputs are finite; a program needn't handle non-finite values.
Results may differ from a plain program's by a relative error of at most 0.0053.
Values may be sent and summed in bfloat16 or wider, within the bound.
A program may use at most 128 MiB of HBM per device.

v0:
```python
import jax
import jax.numpy as jnp
from jax import lax
from jax.sharding import PartitionSpec as P

SCALE = 50.0
EPS = 1e-06


def gelu_back(pre, grad):
    return jax.vjp(jax.nn.gelu, pre)[1](grad)[0]


def on_device(features, w_in, w_out, captions, positive):
    group = ("dp", "row")
    every = ("dp", "row", "col")
    f32 = jnp.float32
    slices = lax.all_to_all(features, group, 1, 0, tiled=True)
    cap32 = captions.astype(f32)
    chat_local = (cap32 * lax.rsqrt(jnp.sum(cap32 * cap32, axis=1, keepdims=True) + EPS)).astype(
        jnp.bfloat16
    )
    chat = lax.all_gather(chat_local, every, axis=0, tiled=True)
    pre = jnp.dot(
        features, lax.all_gather(w_in, "row", axis=0, tiled=True), preferred_element_type=f32
    )
    hidden = jax.nn.gelu(pre).astype(jnp.bfloat16)
    part = jnp.dot(hidden, w_out, preferred_element_type=f32)
    emb = lax.psum_scatter(part, "col", scatter_dimension=0, tiled=True)
    mine = emb.shape[0]
    inv = lax.rsqrt(jnp.sum(emb * emb, axis=1, keepdims=True) + EPS)
    fhat = emb * inv
    fhat_b = fhat.astype(jnp.bfloat16)
    logits = SCALE * lax.dot_general(
        fhat_b, chat, (((1,), (1,)), ((), ())), preferred_element_type=f32
    )
    col = lax.axis_index("col")
    places = lax.dynamic_slice_in_dim(positive, col * mine, mine, 0)
    colids = jnp.arange(chat.shape[0], dtype=jnp.int32)
    mask = (places[:, None] == colids[None, :]).astype(f32)
    expo = jnp.exp(logits)
    picked = mask * logits
    rowsum, rowpos = (jnp.sum(expo, axis=1), jnp.sum(picked, axis=1))
    colsum, colpos = lax.psum((jnp.sum(expo, axis=0), jnp.sum(picked, axis=0)), every)
    fig_terms = lax.all_gather(jnp.log(rowsum) - rowpos, "col", axis=0, tiled=True)
    capdev = captions.shape[0]
    place = (lax.axis_index("dp") * lax.axis_size("row") + lax.axis_index("row")) * lax.axis_size(
        "col"
    ) + col
    cap_terms = lax.dynamic_slice_in_dim(jnp.log(colsum) - colpos, place * capdev, capdev, 0)
    dlog = (expo / rowsum[:, None] + expo / colsum[None, :] - 2.0 * mask).astype(jnp.bfloat16)
    dfhat = SCALE * jnp.dot(dlog, chat, preferred_element_type=f32)
    demb = ((dfhat - fhat * jnp.sum(fhat * dfhat, axis=1, keepdims=True)) * inv).astype(
        jnp.bfloat16
    )
    demb = lax.all_gather(demb, "col", axis=0, tiled=True)
    dh = lax.dot_general(demb, w_out, (((1,), (1,)), ((), ())), preferred_element_type=f32)
    dpre = gelu_back(pre, dh).astype(jnp.bfloat16)
    dpre_all = lax.all_gather(dpre, group, axis=0, tiled=True)
    head_term = lax.dot_general(hidden, demb, (((0,), (0,)), ((), ())), preferred_element_type=f32)
    grad_w_out = lax.psum_scatter(head_term, group, scatter_dimension=1, tiled=True)
    grad_w_in = lax.dot_general(
        slices, dpre_all, (((0,), (0,)), ((), ())), preferred_element_type=f32
    )
    return (fig_terms, cap_terms, grad_w_in, grad_w_out)


def solution(mesh):
    placed = (
        P(("dp", "row"), None),
        P("row", "col"),
        P("col", None),
        P(("dp", "row", "col"), None),
        P(("dp", "row")),
    )
    return jax.shard_map(
        on_device,
        mesh=mesh,
        in_specs=placed,
        out_specs=(
            P(("dp", "row")),
            P(("dp", "row", "col")),
            P(("dp", "row"), "col"),
            P("col", ("dp", "row")),
        ),
        check_vma=False,
    )
```

profile of v0, /device:TPU:0, one launch (start us, length us, event | category | flops | bytes accessed | tf_op | source)
XLA Modules:
  0.0 310.4 jit_solution(15779341503108276041)
XLA Ops:
  8.0 0.0 copy-start
  8.0 0.0 all-gather.4.cloned.1.call-start
  8.1 0.7 all-gather.4.cloned.1.call-update
  8.7 0.0 reduce-scatter.3.cloned.1.call-start
  8.8 24.2 %all-gather.4.cloned.1.call-done = bf16[4096,1024]{1,0:T(8,128)(2,1)} async-done(((bf16[2048,1024]{1,0:T(8,128)(2,1)}), bf16[4096,1024]{1,0:T(8,128)(2,1)}) %all-gather.4.cloned.1.call-update) | async-done | bytes 8388624 | tf_op jit(solution)/shard_map/all_gather | solution.py:25
  33.0 6.3 %fusion.22 = f32[256,1024]{1,0:T(8,128)S(1)} fusion(bf16[256,4096]{1,0:T(8,128)(2,1)} %param.5, bf16[4096,1024]{1,0:T(8,128)(2,1)} %all-gather.4.cloned.1.call-done), kind=kOutput, calls=%fused_computation.43 | convolution fusion | flops 2147483648 | bytes 11534336 | tf_op jit(solution)/shard_map/dot_general | solution.py:24
  39.3 0.0 copy-start.2
  39.3 1.1 copy-done.2
  40.4 0.0 copy-done
  40.4 0.0 copy-start.4
  40.4 0.0 copy-start.5
  40.4 1.8 fusion.21
  42.2 0.0 reduce-scatter.3.cloned.1.call-update
  42.2 0.0 all-gather.6.cloned.1.call-start
  42.3 0.0 copy-done.4
  42.3 0.1 fusion.10
  42.4 0.8 fusion.11
  43.2 0.0 all-gather.6.cloned.1.call-update
  43.2 0.0 all-gather.8.cloned.1.call-start
  43.3 0.0 copy-done.5
  43.3 0.1 dynamic_slice.6
  43.4 28.3 %reduce-scatter.3.cloned.1.call-done = f32[64,1024]{1,0:T(8,128)} async-done(((f32[256,1024]{1,0:T(8,128)}), f32[64,1024]{1,0:T(8,128)}) %reduce-scatter.3.cloned.1.call-update) | async-done | bytes 262160 | tf_op jit(solution)/shard_map/reduce_scatter | solution.py:29
  71.6 1.1 multiply_reduce_fusion.1
  72.7 0.0 copy-start.1
  72.7 36.8 %all-gather.6.cloned.1.call-done = bf16[2048,1024]{1,0:T(8,128)(2,1)} async-done(((bf16[64,1024]{1,0:T(8,128)(2,1)}), bf16[2048,1024]{1,0:T(8,128)(2,1)}) %all-gather.6.cloned.1.call-update) | async-done | bytes 4194320 | tf_op jit(solution)/shard_map/all_gather | solution.py:23
  109.5 3.9 %fusion.8 = (f32[2048]{0:T(1024)S(1)}, f32[64]{0:T(128)S(1)}, f32[2048]{0:T(1024)S(1)}, f32[64]{0:T(128)S(1)}, f32[64,2048]{1,0:T(8,128)S(1)}) fusion(s32[64]{0:T(128)S(1)} %dynamic_slice.6, bf16[2048,1024]{1,0:T(8,128)(2,1)} %all-gather.6.cloned.1.call-done, f32[64,1024]{1,0:T(8,128)} %reduce-scatter.3.cloned.1.call-done, f32[64]{0:T(128)S(1)} %add_rsqrt_fusion.1), kind=kOutput, calls=%fused_computation.16 | convolution fusion | flops 269479808 | bytes 4998144 | tf_op jit(solution)/shard_map/dot_general | solution.py:34
  113.4 39.3 %all-reduce.1 = (f32[2048]{0:T(1024)S(1)}, f32[2048]{0:T(1024)S(1)}) all-reduce(f32[2048]{0:T(1024)S(1)} %get-tuple-element.16, f32[2048]{0:T(1024)S(1)} %get-tuple-element.18), channel_id=1, replica_groups=mesh['dp'=4,'row'=2,'col'=4] {'dp','row','col'}, use_global_device_ids=true, to_apply=%region_8.0 | all-reduce | flops 4096 | bytes 32768 | tf_op jit(solution)/shard_map/psum | solution.py:44
  152.7 0.0 copy-done.1
  152.7 0.0 copy-start.3
  152.7 3.3 %multiply_reduce_fusion = (f32[64]{0:T(128)S(1)}, f32[64,1024]{1,0:T(8,128)S(1)}) fusion(f32[64,1024]{1,0:T(8,128)S(1)} %copy-done.1, f32[64]{0:T(128)S(1)} %add_rsqrt_fusion.1, bf16[2048,1024]{1,0:T(8,128)(2,1)} %all-gather.6.cloned.1.call-done, f32[64,2048]{1,0:T(8,128)S(1)} %get-tuple-element.22, f32[2048]{0:T(1024)S(1)} %get-tuple-element.21, ...), kind=kOutput, calls=%fused_computation.25 | convolution fusion | flops 269615040 | bytes 5252096 | tf_op jit(solution)/shard_map/dot_general | solution.py:52
  156.0 0.1 multiply_convert_fusion.1
  156.1 11.6 %all_gather.18 = bf16[256,1024]{1,0:T(8,128)(2,1)S(1)} all-gather(bf16[64,1024]{1,0:T(8,128)(2,1)S(1)} %multiply_convert_fusion.1), channel_id=1, replica_groups=mesh['dp'=4,'row'=2,'col'=4] {'col'}, dimensions={0}, use_global_device_ids=true | all-gather | bytes 655360 | tf_op jit(solution)/shard_map/all_gather | solution.py:56
  167.7 0.0 copy-done.3
  167.7 2.1 fusion.6
  169.8 0.0 all-gather.8.cloned.1.call-update
  169.8 0.0 reduce-scatter.5.cloned.1.call-start
  169.9 4.0 %fusion.20 = f32[1024,1024]{1,0:T(8,128)} fusion(bf16[256,1024]{1,0:T(8,128)(2,1)S(1)} %all_gather.18, f32[256,1024]{1,0:T(8,128)} %copy-done.2), kind=kOutput, calls=%fused_computation.41 | convolution fusion | flops 539230208 | bytes 5767168 | tf_op jit(solution)/shard_map/dot_general | solution.py:60
  173.9 0.0 reduce-scatter.5.cloned.1.call-update
  173.9 4.1 %copy.11 = bf16[256,4096]{0,1:T(8,128)(2,1)} copy(bf16[256,4096]{1,0:T(8,128)(2,1)} %param.5) | data formatting | bytes 4194304 | tf_op args[0]
  178.1 0.0 copy-start.6
  178.1 4.5 %all-to-all-start = ((bf16[256,8,512]{0,2,1:T(8,128)(2,1)}), bf16[256,8,512]{0,2,1:T(8,128)(2,1)}, u32[]{:S(2)}, u32[]{:S(2)}) async-start(bf16[256,8,512]{0,2,1:T(8,128)(2,1)} %bitcast.16), calls=%async_computation.1 | async-start | bytes 4194304 | tf_op jit(solution)/shard_map/all_to_all | solution.py:18
  182.6 0.0 copy-done.6
  182.6 0.6 dynamic-slice
  183.8 74.7 %all-to-all-done = bf16[256,8,512]{0,2,1:T(8,128)(2,1)} async-done(((bf16[256,8,512]{0,2,1:T(8,128)(2,1)}), bf16[256,8,512]{0,2,1:T(8,128)(2,1)}, u32[]{:S(2)}, u32[]{:S(2)}) %all-to-all-start) | async-done | bytes 2097184 | tf_op jit(solution)/shard_map/all_to_all | solution.py:18
  258.5 4.0 %copy.12 = bf16[8,256,512]{2,1,0:T(8,128)(2,1)} copy(bf16[8,256,512]{1,2,0:T(8,128)(2,1)} %bitcast.2) | data formatting | bytes 4194304 | tf_op jit(solution)/shard_map/all_to_all | solution.py:18
  262.5 0.1 subtract_dynamic-update-slice_fusion
  262.6 10.5 %all-reduce = f32[256]{0:T(256)} all-reduce(f32[256]{0:T(256)S(1)} %subtract_dynamic-update-slice_fusion), channel_id=1, replica_groups=mesh['dp'=4,'row'=2,'col'=4] {'col'}, use_global_device_ids=true, to_apply=%add | all-reduce | flops 256 | bytes 2048
  273.1 0.6 dynamic-slice_subtract_fusion
  273.7 0.0 all-gather.8.cloned.1.call-done
  273.7 6.7 %convolution_bitcast_fusion = f32[512,1024]{0,1:T(8,128)} fusion(bf16[2048,1024]{1,0:T(8,128)(2,1)} %all-gather.8.cloned.1.call-done, bf16[2048,512]{1,0:T(8,128)(2,1)} %bitcast.17), kind=kOutput, calls=%fused_computation.1 | convolution fusion | flops 2147483648 | bytes 8388608 | tf_op jit(solution)/shard_map/dot_general | solution.py:62
  280.4 2.9 copy.13
  283.3 19.6 %reduce-scatter.5.cloned.1.call-done = f32[1024,128]{1,0:T(8,128)} async-done(((f32[1024,1024]{1,0:T(8,128)}), f32[1024,128]{1,0:T(8,128)}) %reduce-scatter.5.cloned.1.call-update) | async-done | bytes 524304 | tf_op jit(solution)/shard_map/reduce_scatter | solution.py:61
  (3 shorter events, 0.0 us)
Async XLA Ops:
  8.0 32.4 %copy-start = (bf16[1024,1024]{1,0:T(8,128)(2,1)S(1)}, bf16[1024,1024]{1,0:T(8,128)(2,1)}, u32[]{:S(2)}) copy-start(bf16[1024,1024]{1,0:T(8,128)(2,1)} %param.7) | copy-start | bytes 6291460
  8.0 25.0 %all-gather.4.cloned.1.call-start = ((), (), s32[]{:S(2)}) async-start(), calls=%async_computation.3 | async-start | bytes 12582912 | tf_op jit(solution)/shard_map/all_gather | solution.py:25
  8.7 62.9 %reduce-scatter.3.cloned.1.call-start = ((), (), s32[]{:S(2)}) async-start(), calls=%async_computation.4 | async-start | bytes 1310720 | tf_op jit(solution)/shard_map/reduce_scatter | solution.py:29
  39.3 1.1 copy-start.2
  40.4 1.9 copy-start.4
  40.4 2.9 copy-start.5
  42.2 67.3 %all-gather.6.cloned.1.call-start = ((), (), s32[]{:S(2)}) async-start(), calls=%async_computation.5 | async-start | bytes 4325376 | tf_op jit(solution)/shard_map/all_gather | solution.py:23
  43.2 230.5 %all-gather.8.cloned.1.call-start = ((), (), s32[]{:S(2)}) async-start(), calls=%async_computation.6 | async-start | bytes 4718592 | tf_op jit(solution)/shard_map/all_gather | solution.py:59
  72.7 80.0 %copy-start.1 = (f32[64,1024]{1,0:T(8,128)S(1)}, f32[64,1024]{1,0:T(8,128)}, u32[]{:S(2)}) copy-start(f32[64,1024]{1,0:T(8,128)} %reduce-scatter.3.cloned.1.call-done) | copy-start | bytes 786436
  152.7 15.0 %copy-start.3 = (f32[256,1024]{1,0:T(8,128)S(1)}, f32[256,1024]{1,0:T(8,128)}, u32[]{:S(2)}) copy-start(f32[256,1024]{1,0:T(8,128)} %copy-done.2) | copy-start | bytes 3145732
  169.8 133.0 %reduce-scatter.5.cloned.1.call-start = ((), (), s32[]{:S(2)}) async-start(), calls=%async_computation.7 | async-start | bytes 4718592 | tf_op jit(solution)/shard_map/reduce_scatter | solution.py:61
  178.1 4.5 %copy-start.6 = (u32[32]{0:T(128)S(1)}, u32[32]{0:T(128)}, u32[]{:S(2)}) copy-start(u32[32]{0:T(128)} %constant.49) | copy-start | bytes 388
  178.1 80.4 %all-to-all-start = ((bf16[256,8,512]{0,2,1:T(8,128)(2,1)}), bf16[256,8,512]{0,2,1:T(8,128)(2,1)}, u32[]{:S(2)}, u32[]{:S(2)}) async-start(bf16[256,8,512]{0,2,1:T(8,128)(2,1)} %bitcast.16), calls=%async_computation.1 | async-start | bytes 4194304 | tf_op jit(solution)/shard_map/all_to_all | solution.py:18
Sparse Core Ops, SparseCore 0:
  10.4 22.5 all-gather.3
  42.4 29.2 reduce-scatter.2
Sparse Core Ops, SparseCore 1:
  46.2 63.3 all-gather.5
  169.9 81.1 all-gather.7
  253.9 48.9 reduce-scatter.4
where the time goes:
time: 311 us; the launch traced here: 310 us
  waiting for transfers between devices  184 us (59%)
  blocking collectives  61.4 us (20%)
  matrix products  28.1 us (9%)
  between operations  16.4 us (5%)
  local copies, waits for them, and re-layouts  12.8 us (4%)
  starting transfers between devices  4.7 us (2%)
    all_to_all x1, waiting for transfers between devices, on_device(): slices = lax.all_to_all(features, group, 1, 0, tiled=True)  74.7 us
    psum x1, blocking collectives, on_device(): lax.psum((jnp.sum(expo, axis=0), jnp.sum(picked, axis=0)), every)  39.3 us
    all_gather x1, waiting for transfers between devices, on_device(): chat = lax.all_gather(chat_local, every, axis=0, tiled=True)  36.8 us
    reduce_scatter x1, waiting for transfers between devices, on_device(): emb = lax.psum_scatter(part, 'col', scatter_dimension=0, tiled=True)  28.3 us
    all_gather x1, waiting for transfers between devices, on_device(): lax.all_gather(w_in, 'row', axis=0, tiled=True)  24.2 us
    reduce_scatter x1, waiting for transfers between devices, on_device(): lax.psum_scatter(head_term, group, scatter_dimension=1, tiled=True)  19.6 us
    all_gather x1, blocking collectives, on_device(): demb = lax.all_gather(demb, 'col', axis=0, tiled=True)  11.6 us
    unnamed x1, blocking collectives  10.5 us
  transfers between devices with their start and end apart: 6, of which 5 were waited for; matrix products, arithmetic and copies ran while one was open for 8% of the time, Pallas kernels for 0%

commit v1 on v0

--- a/solution.py
+++ b/solution.py
@@ -53,7 +53,15 @@
     demb = ((dfhat - fhat * jnp.sum(fhat * dfhat, axis=1, keepdims=True)) * inv).astype(
         jnp.bfloat16
     )
-    demb = lax.all_gather(demb, "col", axis=0, tiled=True)
+    inp = demb
+    d_next, wide_out, small = (lax.axis_size("col"), lax.axis_index("col"), inp.shape[0])
+    by_place = tuple((dev_j * d_next if s == 0 else dev_j for s, dev_j in enumerate(inp.shape)))
+    demb = lax.dynamic_update_slice_in_dim(
+        jnp.zeros(by_place, inp.dtype), inp, wide_out * small, axis=0
+    )
+    for num in [*range(1, d_next)]:
+        inp = lax.ppermute(inp, "col", tuple(((s, (s + 1) % d_next) for s in range(d_next))))
+        demb = lax.dynamic_update_slice_in_dim(demb, inp, (wide_out - num) % d_next * small, axis=0)
     dh = lax.dot_general(demb, w_out, (((1,), (1,)), ((), ())), preferred_element_type=f32)
     dpre = gelu_back(pre, dh).astype(jnp.bfloat16)
     dpre_all = lax.all_gather(dpre, group, axis=0, tiled=True)

time: 311 us -> 320 us (1.029)
  waiting for transfers between devices: 184 us -> 200 us
  blocking collectives: 61.4 us -> 49.7 us
  starting transfers between devices: 4.7 us -> 8.42 us
    ppermute x0 -> x3, waiting for transfers between devices: none -> 14.4 us  [on_device(): lax.ppermute(inp, 'col', tuple(((s, (s + 1) % d_next) for s in range(d_ne...]
    all_gather x1 -> x0, blocking collectives: 11.6 us -> none  [on_device(): demb = lax.all_gather(demb, 'col', axis=0, tiled=True)]
    ppermute x0 -> x3, starting transfers between devices: none -> 3.73 us  [on_device(): lax.ppermute(inp, 'col', tuple(((s, (s + 1) % d_next) for s in range(d_ne...]
    unnamed x18 -> x16, local copies, waits for them, and re-layouts: 8.7 us -> 8.71 us
  transfers between devices with their start and end apart: 6 -> 9, of which waited for: 5 -> 8; matrix products, arithmetic and copies ran while one was open for 8% -> 8% of each run, Pallas kernels for 0% -> 0%
where the time goes in v1:
time: 320 us; the launch traced here: 319 us
  waiting for transfers between devices  200 us (62%)
  blocking collectives  49.7 us (16%)
  matrix products  29.2 us (9%)
  between operations  16.5 us (5%)
  local copies, waits for them, and re-layouts  12.8 us (4%)
  starting transfers between devices  8.42 us (3%)
    all_to_all x1, waiting for transfers between devices, on_device(): slices = lax.all_to_all(features, group, 1, 0, tiled=True)  75 us
    psum x1, blocking collectives, on_device(): lax.psum((jnp.sum(expo, axis=0), jnp.sum(picked, axis=0)), every)  39.3 us
    all_gather x1, waiting for transfers between devices, on_device(): chat = lax.all_gather(chat_local, every, axis=0, tiled=True)  36.8 us
    reduce_scatter x1, waiting for transfers between devices, on_device(): emb = lax.psum_scatter(part, 'col', scatter_dimension=0, tiled=True)  28.3 us
    all_gather x1, waiting for transfers between devices, on_device(): lax.all_gather(w_in, 'row', axis=0, tiled=True)  24.2 us
    reduce_scatter x1, waiting for transfers between devices, on_device(): lax.psum_scatter(head_term, group, scatter_dimension=1, tiled=True)  20.7 us
    ppermute x3, waiting for transfers between devices, on_device(): lax.ppermute(inp, 'col', tuple(((s, (s + 1) % d_next) for s in range(d_ne...  14.4 us
    unnamed x1, blocking collectives  10.4 us
  transfers between devices with their start and end apart: 9, of which 8 were waited for; matrix products, arithmetic and copies ran while one was open for 8% of the time, Pallas kernels for 0%

profile of v1, /device:TPU:0, one launch (start us, length us, event | category | flops | bytes accessed | tf_op | source)
XLA Modules:
  0.0 319.5 jit_solution(2114215066944833400)
XLA Ops:
  8.0 0.0 copy-start
  8.0 0.0 all-gather.4.cloned.1.call-start
  8.1 0.7 all-gather.4.cloned.1.call-update
  8.7 0.0 reduce-scatter.3.cloned.1.call-start
  8.8 24.2 %all-gather.4.cloned.1.call-done = bf16[4096,1024]{1,0:T(8,128)(2,1)} async-done(((bf16[2048,1024]{1,0:T(8,128)(2,1)}), bf16[4096,1024]{1,0:T(8,128)(2,1)}) %all-gather.4.cloned.1.call-update) | async-done | bytes 8388624 | tf_op jit(solution)/shard_map/all_gather | solution.py:25
  33.0 6.3 %fusion.22 = f32[256,1024]{1,0:T(8,128)S(1)} fusion(bf16[256,4096]{1,0:T(8,128)(2,1)} %param.5, bf16[4096,1024]{1,0:T(8,128)(2,1)} %all-gather.4.cloned.1.call-done), kind=kOutput, calls=%fused_computation.47 | convolution fusion | flops 2147483648 | bytes 11534336 | tf_op jit(solution)/shard_map/dot_general | solution.py:24
  39.3 0.0 copy-start.2
  39.3 1.1 copy-done.2
  40.4 0.0 copy-done
  40.4 0.0 copy-start.3
  40.4 0.0 copy-start.4
  40.4 1.8 fusion.21
  42.2 0.0 reduce-scatter.3.cloned.1.call-update
  42.2 0.0 all-gather.6.cloned.1.call-start
  42.3 0.0 copy-done.3
  42.3 0.1 fusion.10
  42.4 0.8 fusion.11
  43.2 0.0 all-gather.6.cloned.1.call-update
  43.2 0.0 all-gather.8.cloned.1.call-start
  43.3 0.0 copy-done.4
  43.3 0.1 dynamic_slice.6
  43.4 28.3 %reduce-scatter.3.cloned.1.call-done = f32[64,1024]{1,0:T(8,128)} async-done(((f32[256,1024]{1,0:T(8,128)}), f32[64,1024]{1,0:T(8,128)}) %reduce-scatter.3.cloned.1.call-update) | async-done | bytes 262160 | tf_op jit(solution)/shard_map/reduce_scatter | solution.py:29
  71.6 1.1 multiply_reduce_fusion.1
  72.7 0.0 copy-start.1
  72.7 36.8 %all-gather.6.cloned.1.call-done = bf16[2048,1024]{1,0:T(8,128)(2,1)} async-done(((bf16[64,1024]{1,0:T(8,128)(2,1)}), bf16[2048,1024]{1,0:T(8,128)(2,1)}) %all-gather.6.cloned.1.call-update) | async-done | bytes 4194320 | tf_op jit(solution)/shard_map/all_gather | solution.py:23
  109.5 3.9 %fusion.8 = (f32[2048]{0:T(1024)S(1)}, f32[64]{0:T(128)S(1)}, f32[2048]{0:T(1024)S(1)}, f32[64]{0:T(128)S(1)}, f32[64,2048]{1,0:T(8,128)S(1)}) fusion(s32[64]{0:T(128)S(1)} %dynamic_slice.6, bf16[2048,1024]{1,0:T(8,128)(2,1)} %all-gather.6.cloned.1.call-done, f32[64,1024]{1,0:T(8,128)} %reduce-scatter.3.cloned.1.call-done, f32[64]{0:T(128)S(1)} %add_rsqrt_fusion.1), kind=kOutput, calls=%fused_computation.16 | convolution fusion | flops 269479808 | bytes 4998144 | tf_op jit(solution)/shard_map/dot_general | solution.py:34
  113.4 39.3 %all-reduce.1 = (f32[2048]{0:T(1024)S(1)}, f32[2048]{0:T(1024)S(1)}) all-reduce(f32[2048]{0:T(1024)S(1)} %get-tuple-element.16, f32[2048]{0:T(1024)S(1)} %get-tuple-element.18), channel_id=1, replica_groups=mesh['dp'=4,'row'=2,'col'=4] {'dp','row','col'}, use_global_device_ids=true, to_apply=%region_8.0 | all-reduce | flops 4096 | bytes 32768 | tf_op jit(solution)/shard_map/psum | solution.py:44
  152.7 0.0 copy-done.1
  152.7 3.2 %multiply_reduce_fusion = (f32[64]{0:T(128)S(1)}, f32[64,1024]{1,0:T(8,128)S(1)}) fusion(f32[64,1024]{1,0:T(8,128)S(1)} %copy-done.1, f32[64]{0:T(128)S(1)} %add_rsqrt_fusion.1, bf16[2048,1024]{1,0:T(8,128)(2,1)} %all-gather.6.cloned.1.call-done, f32[64,2048]{1,0:T(8,128)S(1)} %get-tuple-element.24, f32[2048]{0:T(1024)S(1)} %get-tuple-element.21, ...), kind=kOutput, calls=%fused_computation.25 | convolution fusion | flops 269615040 | bytes 5252096 | tf_op jit(solution)/shard_map/dot_general | solution.py:52
  155.9 0.1 broadcast_in_dim.2
  156.0 0.1 constant_dynamic-update-slice_fusion.3
  156.1 2.3 collective-permute-start
  158.4 4.0 %collective-permute-done = bf16[64,1024]{1,0:T(8,128)(2,1)S(1)} collective-permute-done((bf16[64,1024]{1,0:T(8,128)(2,1)S(1)}, bf16[64,1024]{1,0:T(8,128)(2,1)S(1)}, u32[]{:S(2)}, u32[]{:S(2)}) %collective-permute-start) | collective-permute-done | bytes 131104 | tf_op jit(solution)/shard_map/ppermute | solution.py:63
  162.4 1.0 collective-permute-start.1
  163.4 5.0 %collective-permute-done.1 = bf16[64,1024]{1,0:T(8,128)(2,1)S(1)} collective-permute-done((bf16[64,1024]{1,0:T(8,128)(2,1)S(1)}, bf16[64,1024]{1,0:T(8,128)(2,1)S(1)}, u32[]{:S(2)}, u32[]{:S(2)}) %collective-permute-start.1) | collective-permute-done | bytes 131104 | tf_op jit(solution)/shard_map/ppermute | solution.py:63
  168.4 0.4 collective-permute-start.2
  168.8 5.4 %collective-permute-done.2 = bf16[64,1024]{1,0:T(8,128)(2,1)S(1)} collective-permute-done((bf16[64,1024]{1,0:T(8,128)(2,1)S(1)}, bf16[64,1024]{1,0:T(8,128)(2,1)S(1)}, u32[]{:S(2)}, u32[]{:S(2)}) %collective-permute-start.2) | collective-permute-done | bytes 131104 | tf_op jit(solution)/shard_map/ppermute | solution.py:63
  174.3 3.3 %fusion.6 = bf16[256,1024]{1,0:T(8,128)(2,1)} fusion(f32[256,1024]{1,0:T(8,128)} %copy-done.2, bf16[256,1024]{1,0:T(8,128)(2,1)S(1)} %constant_dynamic-update-slice_fusion, bf16[1024,1024]{1,0:T(8,128)(2,1)S(1)} %copy-done), kind=kOutput, calls=%fused_computation.11 | convolution fusion | flops 542113792 | bytes 4194304 | tf_op jit(solution)/shard_map/dot_general | solution.py:65
  177.5 0.0 all-gather.8.cloned.1.call-update
  177.6 0.0 reduce-scatter.5.cloned.1.call-start
  177.6 4.0 %fusion.20 = f32[1024,1024]{1,0:T(8,128)} fusion(bf16[256,1024]{1,0:T(8,128)(2,1)S(1)} %constant_dynamic-update-slice_fusion, f32[256,1024]{1,0:T(8,128)} %copy-done.2), kind=kOutput, calls=%fused_computation.45 | convolution fusion | flops 539230208 | bytes 5767168 | tf_op jit(solution)/shard_map/dot_general | solution.py:68
  181.7 0.0 reduce-scatter.5.cloned.1.call-update
  181.7 4.2 %copy.11 = bf16[256,4096]{0,1:T(8,128)(2,1)} copy(bf16[256,4096]{1,0:T(8,128)(2,1)} %param.5) | data formatting | bytes 4194304 | tf_op args[0]
  185.8 0.0 copy-start.5
  185.8 4.5 %all-to-all-start = ((bf16[256,8,512]{0,2,1:T(8,128)(2,1)}), bf16[256,8,512]{0,2,1:T(8,128)(2,1)}, u32[]{:S(2)}, u32[]{:S(2)}) async-start(bf16[256,8,512]{0,2,1:T(8,128)(2,1)} %bitcast.16), calls=%async_computation.1 | async-start | bytes 4194304 | tf_op jit(solution)/shard_map/all_to_all | solution.py:18
  190.3 0.0 copy-done.5
  190.4 0.6 dynamic-slice
  191.6 75.0 %all-to-all-done = bf16[256,8,512]{0,2,1:T(8,128)(2,1)} async-done(((bf16[256,8,512]{0,2,1:T(8,128)(2,1)}), bf16[256,8,512]{0,2,1:T(8,128)(2,1)}, u32[]{:S(2)}, u32[]{:S(2)}) %all-to-all-start) | async-done | bytes 2097184 | tf_op jit(solution)/shard_map/all_to_all | solution.py:18
  266.6 3.9 %copy.12 = bf16[8,256,512]{2,1,0:T(8,128)(2,1)} copy(bf16[8,256,512]{1,2,0:T(8,128)(2,1)} %bitcast.2) | data formatting | bytes 4194304 | tf_op jit(solution)/shard_map/all_to_all | solution.py:18
  270.5 0.1 subtract_dynamic-update-slice_fusion
  270.6 10.4 %all-reduce = f32[256]{0:T(256)} all-reduce(f32[256]{0:T(256)S(1)} %subtract_dynamic-update-slice_fusion), channel_id=1, replica_groups=mesh['dp'=4,'row'=2,'col'=4] {'col'}, use_global_device_ids=true, to_apply=%add | all-reduce | flops 256 | bytes 2048
  281.0 0.6 dynamic-slice_subtract_fusion
  281.6 0.0 all-gather.8.cloned.1.call-done
  281.6 6.7 %convolution_bitcast_fusion = f32[512,1024]{0,1:T(8,128)} fusion(bf16[2048,1024]{1,0:T(8,128)(2,1)} %all-gather.8.cloned.1.call-done, bf16[2048,512]{1,0:T(8,128)(2,1)} %bitcast.17), kind=kOutput, calls=%fused_computation.1 | convolution fusion | flops 2147483648 | bytes 8388608 | tf_op jit(solution)/shard_map/dot_general | solution.py:70
  288.3 2.9 copy.13
  291.2 20.7 %reduce-scatter.5.cloned.1.call-done = f32[1024,128]{1,0:T(8,128)} async-done(((f32[1024,1024]{1,0:T(8,128)}), f32[1024,128]{1,0:T(8,128)}) %reduce-scatter.5.cloned.1.call-update) | async-done | bytes 524304 | tf_op jit(solution)/shard_map/reduce_scatter | solution.py:69
  (6 shorter events, 0.1 us)
Async XLA Ops:
  8.0 32.4 %copy-start = (bf16[1024,1024]{1,0:T(8,128)(2,1)S(1)}, bf16[1024,1024]{1,0:T(8,128)(2,1)}, u32[]{:S(2)}) copy-start(bf16[1024,1024]{1,0:T(8,128)(2,1)} %param.7) | copy-start | bytes 6291460
  8.0 25.0 %all-gather.4.cloned.1.call-start = ((), (), s32[]{:S(2)}) async-start(), calls=%async_computation.3 | async-start | bytes 12582912 | tf_op jit(solution)/shard_map/all_gather | solution.py:25
  8.7 62.9 %reduce-scatter.3.cloned.1.call-start = ((), (), s32[]{:S(2)}) async-start(), calls=%async_computation.4 | async-start | bytes 1310720 | tf_op jit(solution)/shard_map/reduce_scatter | solution.py:29
  39.3 1.1 copy-start.2
  40.4 1.9 copy-start.3
  40.4 2.9 copy-start.4
  42.2 67.3 %all-gather.6.cloned.1.call-start = ((), (), s32[]{:S(2)}) async-start(), calls=%async_computation.5 | async-start | bytes 4325376 | tf_op jit(solution)/shard_map/all_gather | solution.py:23
  43.2 238.4 %all-gather.8.cloned.1.call-start = ((), (), s32[]{:S(2)}) async-start(), calls=%async_computation.6 | async-start | bytes 4718592 | tf_op jit(solution)/shard_map/all_gather | solution.py:67
  72.7 80.0 %copy-start.1 = (f32[64,1024]{1,0:T(8,128)S(1)}, f32[64,1024]{1,0:T(8,128)}, u32[]{:S(2)}) copy-start(f32[64,1024]{1,0:T(8,128)} %reduce-scatter.3.cloned.1.call-done) | copy-start | bytes 786436
  156.1 6.3 %collective-permute-start = (bf16[64,1024]{1,0:T(8,128)(2,1)S(1)}, bf16[64,1024]{1,0:T(8,128)(2,1)S(1)}, u32[]{:S(2)}, u32[]{:S(2)}) collective-permute-start(bf16[64,1024]{1,0:T(8,128)(2,1)S(1)} %get-tuple-element.23), channel_id=1, source_target_pairs={{0,1},{1,2},{2,3},{3,0},{4,5},{5,6},{6,7},{7,4},{8,9},{9,10},{10,1... | collective-permute-start | bytes 393224 | tf_op jit(solution)/shard_map/ppermute | solution.py:63
  162.4 6.0 %collective-permute-start.1 = (bf16[64,1024]{1,0:T(8,128)(2,1)S(1)}, bf16[64,1024]{1,0:T(8,128)(2,1)S(1)}, u32[]{:S(2)}, u32[]{:S(2)}) collective-permute-start(bf16[64,1024]{1,0:T(8,128)(2,1)S(1)} %collective-permute-done), channel_id=1, source_target_pairs={{0,1},{1,2},{2,3},{3,0},{4,5},{5,6},{6,7},{7,4},{8,9},{9,10},{10,1... | collective-permute-start | bytes 393224 | tf_op jit(solution)/shard_map/ppermute | solution.py:63
  168.4 5.9 %collective-permute-start.2 = (bf16[64,1024]{1,0:T(8,128)(2,1)S(1)}, bf16[64,1024]{1,0:T(8,128)(2,1)S(1)}, u32[]{:S(2)}, u32[]{:S(2)}) collective-permute-start(bf16[64,1024]{1,0:T(8,128)(2,1)S(1)} %collective-permute-done.1), channel_id=1, source_target_pairs={{0,1},{1,2},{2,3},{3,0},{4,5},{5,6},{6,7},{7,4},{8,9},{9,10},{10,1... | collective-permute-start | bytes 393224 | tf_op jit(solution)/shard_map/ppermute | solution.py:63
  177.6 134.4 %reduce-scatter.5.cloned.1.call-start = ((), (), s32[]{:S(2)}) async-start(), calls=%async_computation.7 | async-start | bytes 4718592 | tf_op jit(solution)/shard_map/reduce_scatter | solution.py:69
  185.8 4.5 %copy-start.5 = (u32[32]{0:T(128)S(1)}, u32[32]{0:T(128)}, u32[]{:S(2)}) copy-start(u32[32]{0:T(128)} %constant.77) | copy-start | bytes 388
  185.8 80.8 %all-to-all-start = ((bf16[256,8,512]{0,2,1:T(8,128)(2,1)}), bf16[256,8,512]{0,2,1:T(8,128)(2,1)}, u32[]{:S(2)}, u32[]{:S(2)}) async-start(bf16[256,8,512]{0,2,1:T(8,128)(2,1)} %bitcast.16), calls=%async_computation.1 | async-start | bytes 4194304 | tf_op jit(solution)/shard_map/all_to_all | solution.py:18
Sparse Core Ops, SparseCore 0:
  10.4 22.5 all-gather.3
  42.4 29.2 reduce-scatter.2
Sparse Core Ops, SparseCore 1:
  46.2 63.3 all-gather.5
  177.6 81.6 all-gather.7
  262.1 49.7 reduce-scatter.4
